TPU v7x, 32 devices: a whole 2x2x4 slice. The times are simulated.
32 devices in a mesh: dp: 8 (over z, x), pipe: 2 (over y), tensor: 2 (over core).
Axes of the slice: x: 2, y: 2, z: 4, core: 2. Of those that a mesh axis runs over, the one named last changes fastest.
Arguments:
- query_states: bfloat16 [2, 512, 4096], P('pipe', 'dp', 'tensor'), may hold values from -6 to 6
- passage_hidden_states: bfloat16 [2, 1440, 4096], P('pipe', 'dp', 'tensor'), may hold values from -6 to 6
- w_query: bfloat16 [2, 4096, 4096], P('pipe', 'dp', 'tensor'), may hold values from -0.09375 to 0.09375
- key_matrix: bfloat16 [2, 4096, 1024], P('pipe', 'dp', 'tensor'), may hold values from -0.09375 to 0.09375
- value_matrix: bfloat16 [2, 4096, 1024], P('pipe', 'dp', 'tensor'), may hold values from -0.09375 to 0.09375
- w_out: bfloat16 [2, 4096, 4096], P('pipe', 'tensor', 'dp'), may hold values from -0.09375 to 0.09375
- final_gain: bfloat16 [4096], P('tensor'), may hold values from 0.5 to 2
- w_vector: bfloat16 [4096, 128], P('tensor'), may hold values from -0.09375 to 0.09375
- lengths: int32 [8], P('dp'), may hold values from 1 to 180, 896 in all
- teacher: float32 [16, 8], P(('dp', 'pipe')), may hold values from -12 to 12
Outputs:
- boundary_queries: bfloat16 [2, 512, 4096], P('pipe', 'dp', 'tensor')
- boundary_passages: bfloat16 [2, 1440, 4096], P('pipe', 'dp', 'tensor')
- scores: float32 [16, 8], P(('dp', 'pipe'))
- divergence: float32 [16], P(('dp', 'pipe'))
Inputs may be any that keep to these rules, and one draw needn't show every extreme that they name: Each passage's valid tokens come first; slots after lengths[p] are padding. Some passage fills all 180 slots.
All inputs are finite; a program needn't handle non-finite values. No bound on the sum of `lengths` on one device may be relied on, other than what follows from the above.
Results may differ from a plain program's by a relative error of at most 0.0075.
Values may be sent and summed in bfloat16 or wider, within the bound.
A program may use at most 128 MiB of HBM per device.

v0:
```python
import jax
import jax.numpy as jnp
from jax import lax
from jax.sharding import PartitionSpec as P

MODEL_WIDTH = 4096
HEAD_WIDTH = 128
VEC = 128
QLEN = 32
PLEN = 180
norm_epsilon = 1e-05
vector_epsilon = 1e-06
rope_base = 10000.0


def from_root(array, axis, root):
    mine = lax.axis_index(axis) == root
    return lax.psum(jnp.where(mine, array, jnp.zeros_like(array)), axis)


def rotate(values_in, positions):
    half_size = values_in.shape[-1] // 2
    frequency = rope_base ** (-jnp.arange(half_size).astype(jnp.float32) / half_size)
    angles = positions.astype(jnp.float32)[:, None] * frequency[None, :]
    cosine = jnp.cos(angles)[:, None, :]
    sine = jnp.sin(angles)[:, None, :]
    first_half = values_in[..., :half_size]
    second_half = values_in[..., half_size:]
    return jnp.concatenate(
        [first_half * cosine - second_half * sine, second_half * cosine + first_half * sine],
        axis=-1,
    )


def attend(queries, keys, values_in):
    batch_count, length, head_count, head_size = queries.shape
    key_heads = keys.shape[2]
    grouped = queries.reshape(batch_count, length, key_heads, head_count // key_heads, head_size)
    logits = jnp.einsum(
        "bskgd,bukd->bkgsu", grouped, keys, preferred_element_type=jnp.float32
    ) * head_size ** (-0.5)
    causal = jnp.arange(length)[:, None] >= jnp.arange(length)[None, :]
    weights = jnp.where(causal, jnp.exp(logits), 0.0)
    probability = (weights / jnp.sum(weights, axis=-1, keepdims=True)).astype(jnp.bfloat16)
    combined = jnp.einsum(
        "bkgsu,bukd->bskgd", probability, values_in, preferred_element_type=jnp.float32
    )
    return combined.reshape(batch_count * length, head_count * head_size).astype(jnp.bfloat16)


def by_sequence(array_in, head_number, seq_length):
    return array_in.reshape(-1, seq_length, head_number, HEAD_WIDTH)


def late_scores(query_vectors, passage_vectors, passage_lengths):
    sims = jnp.einsum(
        "qtc,psc->qtps", query_vectors, passage_vectors, preferred_element_type=jnp.float32
    )
    valid = jnp.arange(passage_vectors.shape[1])[None, :] < passage_lengths[:, None]
    masked = jnp.where(valid[None, None], sims, -3.0)
    return jnp.sum(jnp.max(masked, axis=3), axis=1)


def body(
    query_states,
    passage_hidden_states,
    w_query,
    key_matrix,
    value_matrix,
    w_out,
    final_gain,
    w_vector,
    lengths,
    teacher,
):
    query_rows = query_states[0]
    passage_rows = passage_hidden_states[0]
    query_count = query_rows.shape[0]
    joined = jnp.concatenate([query_rows, passage_rows], axis=0)
    widened = joined.astype(jnp.float32)
    squares = jnp.sum(widened * widened, axis=1)
    total = lax.psum(squares, "tensor")
    normed_local = (widened * lax.rsqrt(total / MODEL_WIDTH + norm_epsilon)[:, None]).astype(
        jnp.bfloat16
    )
    normed = lax.all_gather(normed_local, "tensor", axis=1, tiled=True)
    query_cols = w_query.shape[2]
    key_cols = key_matrix.shape[2]
    pieces = (
        lax.all_gather(w_query[0], "dp", axis=0, tiled=True),
        lax.all_gather(key_matrix[0], "dp", axis=0, tiled=True),
        lax.all_gather(value_matrix[0], "dp", axis=0, tiled=True),
    )
    queries, keys, unprojected_values = tuple(
        (jnp.dot(normed, piece, preferred_element_type=jnp.float32) for piece in pieces)
    )
    values_out = unprojected_values.astype(jnp.bfloat16)
    query_heads = query_cols // HEAD_WIDTH
    key_heads = key_cols // HEAD_WIDTH
    query_pos = jnp.arange(QLEN)
    passage_pos = jnp.arange(PLEN)
    short_q = rotate(by_sequence(queries[:query_count], query_heads, QLEN), query_pos).astype(
        jnp.bfloat16
    )
    short_k = rotate(by_sequence(keys[:query_count], key_heads, QLEN), query_pos).astype(
        jnp.bfloat16
    )
    short_v = by_sequence(values_out[:query_count], key_heads, QLEN)
    long_q = rotate(by_sequence(queries[query_count:], query_heads, PLEN), passage_pos).astype(
        jnp.bfloat16
    )
    long_k = rotate(by_sequence(keys[query_count:], key_heads, PLEN), passage_pos).astype(
        jnp.bfloat16
    )
    long_v = by_sequence(values_out[query_count:], key_heads, PLEN)
    attended = jnp.concatenate(
        [attend(short_q, short_k, short_v), attend(long_q, long_k, long_v)], axis=0
    )
    branch_full = jnp.dot(
        attended,
        lax.all_gather(w_out[0], "dp", axis=1, tiled=True),
        preferred_element_type=jnp.float32,
    )
    branch = lax.psum_scatter(
        branch_full.astype(jnp.bfloat16), "tensor", scatter_dimension=1, tiled=True
    ).astype(jnp.float32)
    updated = (widened + branch).astype(jnp.bfloat16)
    boundary_queries = updated[:query_count][None]
    boundary_passages = updated[query_count:][None]
    scaled = (updated.astype(jnp.float32) * final_gain.astype(jnp.float32)[None, :]).astype(
        jnp.bfloat16
    )
    partial_vec = jnp.dot(scaled, w_vector, preferred_element_type=jnp.float32)
    projected = lax.psum(partial_vec.astype(jnp.bfloat16), "tensor").astype(jnp.float32)
    vectors = (
        projected
        * lax.rsqrt(jnp.sum(projected * projected, axis=1, keepdims=True) + vector_epsilon)
    ).astype(jnp.bfloat16)
    query_vectors = vectors[:query_count].reshape(-1, QLEN, VEC)
    passage_vectors = vectors[query_count:].reshape(-1, PLEN, VEC)
    last_section = lax.axis_size("pipe") - 1
    query_vectors, passage_vectors = (
        from_root(query_vectors, "pipe", last_section),
        from_root(passage_vectors, "pipe", last_section),
    )
    owned = query_vectors.shape[0] // lax.axis_size("pipe")
    own_queries = lax.dynamic_slice_in_dim(query_vectors, lax.axis_index("pipe") * owned, owned, 0)
    pieces = (
        lax.all_gather(passage_vectors, "dp", axis=0, tiled=True),
        lax.all_gather(lengths, "dp", axis=0, tiled=True),
    )
    block = late_scores(own_queries, pieces[0], pieces[1])
    log_student = block - jnp.log(jnp.sum(jnp.exp(block), axis=1, keepdims=True))
    log_teacher = teacher - jnp.log(jnp.sum(jnp.exp(teacher), axis=1, keepdims=True))
    divergence = jnp.sum(jnp.exp(log_teacher) * (log_teacher - log_student), axis=1)
    return (boundary_queries, boundary_passages, block, divergence)


def solution(mesh):
    in_specs = (
        P("pipe", "dp", "tensor"),
        P("pipe", "dp", "tensor"),
        P("pipe", "dp", "tensor"),
        P("pipe", "dp", "tensor"),
        P("pipe", "dp", "tensor"),
        P("pipe", "tensor", "dp"),
        P("tensor"),
        P("tensor", None),
        P("dp"),
        P(("dp", "pipe"), None),
    )
    out_specs = (
        P("pipe", "dp", "tensor"),
        P("pipe", "dp", "tensor"),
        P(("dp", "pipe"), None),
        P(("dp", "pipe")),
    )
    return jax.shard_map(body, mesh=mesh, in_specs=in_specs, out_specs=out_specs, check_vma=False)
```

profile of v0, /device:TPU:0, one launch (start us, length us, event | category | flops | bytes accessed | tf_op | source)
XLA Modules:
  0.0 714.7 jit_solution(4791329132297808971)
XLA Ops:
  7.2 1.5 fusion.12
  8.7 2.6 psum.28
  11.3 2.4 fusion.13
  17.1 9.9 %all-gather.10.cloned.1.call-done = bf16[244,4096]{1,0:T(8,128)(2,1)} async-done(((bf16[244,2048]{1,0:T(8,128)(2,1)}), bf16[244,4096]{1,0:T(8,128)(2,1)}) %all-gather.10.cloned.1.call-update) | async-done | bytes 1998864 | tf_op jit(solution)/shard_map/all_gather | solution.py:86
  26.9 76.7 %all-gather.14.cloned.1.call-done = bf16[1,4096,512]{2,1,0:T(8,128)(2,1)} async-done(((bf16[1,512,512]{2,1,0:T(8,128)(2,1)}), bf16[1,4096,512]{2,1,0:T(8,128)(2,1)}) %all-gather.14.cloned.1.call-update) | async-done | bytes 4194320 | tf_op jit(solution)/shard_map/all_gather | solution.py:91
  103.7 4.0 fusion.7
  107.7 69.8 %all-gather.12.cloned.1.call-done = bf16[1,4096,512]{2,1,0:T(8,128)(2,1)} async-done(((bf16[1,512,512]{2,1,0:T(8,128)(2,1)}), bf16[1,4096,512]{2,1,0:T(8,128)(2,1)}) %all-gather.12.cloned.1.call-update) | async-done | bytes 4194320 | tf_op jit(solution)/shard_map/all_gather | solution.py:92
  177.5 4.0 fusion.27
  181.7 0.7 reshape.283
  183.0 222.4 %all-gather.16.cloned.1.call-done = bf16[1,4096,2048]{2,1,0:T(8,128)(2,1)} async-done(((bf16[1,512,2048]{2,1,0:T(8,128)(2,1)}), bf16[1,4096,2048]{2,1,0:T(8,128)(2,1)}) %all-gather.16.cloned.1.call-update) | async-done | bytes 16777232 | tf_op jit(solution)/shard_map/all_gather | solution.py:90
  405.4 8.6 %fusion.2 = f32[244,2048]{1,0:T(8,128)S(1)} fusion(bf16[244,4096]{1,0:T(8,128)(2,1)} %all-gather.10.cloned.1.call-done, bf16[1,4096,2048]{2,1,0:T(8,128)(2,1)} %all-gather.16.cloned.1.call-done), kind=kOutput, calls=%fused_computation.2 | convolution fusion | flops 4093640704 | bytes 20774912 | tf_op jit(solution)/shard_map/dot_general | solution.py:95
  415.7 1.3 fusion.11
  417.0 1.0 fusion.21
  418.3 1.3 convert_element_type.173
  421.4 211.9 %all-gather.18.cloned.1.call-done = bf16[1,2048,4096]{2,1,0:T(8,128)(2,1)} async-done(((bf16[1,2048,512]{2,1,0:T(8,128)(2,1)}), bf16[1,2048,4096]{2,1,0:T(8,128)(2,1)}) %all-gather.18.cloned.1.call-update) | async-done | bytes 16777232 | tf_op jit(solution)/shard_map/all_gather | solution.py:121
  633.2 11.6 %fusion.4 = bf16[244,4096]{1,0:T(8,128)(2,1)} fusion(bf16[1,2048,4096]{2,1,0:T(8,128)(2,1)} %all-gather.18.cloned.1.call-done, bf16[180,2048]{1,0:T(8,128)(2,1)S(1)} %copy-done.3, bf16[64,2048]{1,0:T(8,128)(2,1)S(1)} %convert_element_type.167), kind=kOutput, calls=%fused_computation.4 | convolution fusion | flops 4096638976 | bytes 19775488 | tf_op jit(solution)/shard_map/dot_general | solution.py:119
  646.2 0.8 dynamic-update-slice
  647.0 9.5 %all-reduce = s32[8]{0:T(128)S(1)} all-reduce(s32[8]{0:T(128)S(1)} %dynamic-update-slice), channel_id=1, replica_groups=mesh['dp'=8,'pipe'=2,'tensor'=2] {'dp'}, use_global_device_ids=true, to_apply=%add | all-reduce | flops 8 | bytes 64
  657.9 1.6 fusion.14
  659.9 3.6 psum.29
  663.8 0.9 slice_bitcast_fusion.1
  664.7 0.7 slice_bitcast_fusion.3
  665.4 8.8 %all-reduce.1 = (bf16[1,180,128]{2,1,0:T(8,128)(2,1)S(1)}, bf16[2,32,128]{2,1,0:T(8,128)(2,1)S(1)}) all-reduce(bf16[1,180,128]{2,1,0:T(8,128)(2,1)S(1)} %fusion.54, bf16[2,32,128]{2,1,0:T(8,128)(2,1)S(1)} %bitcast.117), channel_id=1, replica_groups=mesh['dp'=8,'pipe'=2,'tensor'=2] {'pipe'}, use_global_device_ids=true, to_apply=%region_8.9 | all-reduce | flops 31232 | bytes 124928 | tf_op jit(solution)/shard_map/psum | solution.py:18
  674.2 31.2 %all_gather.27 = bf16[8,180,128]{2,1,0:T(8,128)(2,1)S(1)} all-gather(bf16[1,180,128]{2,1,0:T(8,128)(2,1)S(1)} %get-tuple-element.4), channel_id=1, replica_groups=mesh['dp'=8,'pipe'=2,'tensor'=2] {'dp'}, dimensions={0}, use_global_device_ids=true | all-gather | bytes 414720 | tf_op jit(solution)/shard_map/all_gather | solution.py:149
  (81 shorter events, 11.4 us)
Async XLA Ops:
  7.2 652.3 %copy-start = (bf16[2048,128]{1,0:T(8,128)(2,1)S(1)}, bf16[2048,128]{1,0:T(8,128)(2,1)}, u32[]{:S(2)}) copy-start(bf16[2048,128]{1,0:T(8,128)(2,1)} %param.17) | copy-start | bytes 1572868
  7.2 19.8 %all-gather.10.cloned.1.call-start = ((), (), s32[]{:S(2)}) async-start(), calls=%async_computation.1 | async-start | bytes 3047424 | tf_op jit(solution)/shard_map/all_gather | solution.py:86
  13.7 89.9 %all-gather.14.cloned.1.call-start = ((), (), s32[]{:S(2)}) async-start(), calls=%async_computation.4 | async-start | bytes 4718592 | tf_op jit(solution)/shard_map/all_gather | solution.py:91
  14.5 163.0 %all-gather.12.cloned.1.call-start = ((), (), s32[]{:S(2)}) async-start(), calls=%async_computation.3 | async-start | bytes 4718592 | tf_op jit(solution)/shard_map/all_gather | solution.py:92
  15.2 390.2 %all-gather.16.cloned.1.call-start = ((), (), s32[]{:S(2)}) async-start(), calls=%async_computation.5 | async-start | bytes 18874368 | tf_op jit(solution)/shard_map/all_gather | solution.py:90
  15.8 617.5 %all-gather.18.cloned.1.call-start = ((), (), s32[]{:S(2)}) async-start(), calls=%async_computation.6 | async-start | bytes 18874368 | tf_op jit(solution)/shard_map/all_gather | solution.py:121
  16.4 641.5 %reduce-scatter.2.cloned.1.call-start = ((), (), s32[]{:S(2)}) async-start(), calls=%async_computation.2 | async-start | bytes 3047424 | tf_op jit(solution)/shard_map/reduce_scatter | solution.py:124
  415.6 1.3 copy-start.4
  420.1 213.1 %copy-start.3 = (bf16[180,2048]{1,0:T(8,128)(2,1)S(1)}, bf16[180,2048]{1,0:T(8,128)(2,1)}, u32[]{:S(2)}) copy-start(bf16[180,2048]{1,0:T(8,128)(2,1)} %convert_element_type.173) | copy-start | bytes 2211844
  644.9 0.8 copy-start.8
  644.9 11.6 %copy-start.5 = (bf16[2048]{0:T(1024)(128)(2,1)S(1)}, bf16[2048]{0:T(1024)(128)(2,1)}, u32[]{:S(2)}) copy-start(bf16[2048]{0:T(1024)(128)(2,1)} %param.16) | copy-start | bytes 12292
  644.9 11.6 %copy-start.7 = (f32[1,8]{1,0:T(1,128)S(1)}, f32[1,8]{1,0:T(1,128)}, u32[]{:S(2)}) copy-start(f32[1,8]{1,0:T(1,128)} %param.19) | copy-start | bytes 100
  644.9 13.0 %copy-start.1 = (bf16[1,180,2048]{2,1,0:T(8,128)(2,1)S(1)}, bf16[1,180,2048]{2,1,0:T(8,128)(2,1)}, u32[]{:S(2)}) copy-start(bf16[1,180,2048]{2,1,0:T(8,128)(2,1)} %param.11) | copy-start | bytes 2211844
  644.9 13.0 %copy-start.2 = (bf16[1,64,2048]{2,1,0:T(8,128)(2,1)S(1)}, bf16[1,64,2048]{2,1,0:T(8,128)(2,1)}, u32[]{:S(2)}) copy-start(bf16[1,64,2048]{2,1,0:T(8,128)(2,1)} %param.10) | copy-start | bytes 786436
  705.9 1.9 copy-start.6
Sparse Core Ops, SparseCore 0:
  13.8 13.0 all-gather.9
  29.1 74.5 all-gather.13
  105.8 71.6 all-gather.11
  179.5 225.8 all-gather.15
  407.3 225.9 all-gather.17
  645.0 7.7 reduce-scatter.1
where the time goes:
time: 715 us
  waiting for transfers between devices  593 us (83%)
  blocking collectives  55.6 us (8%)
  matrix products  32.3 us (5%)
  between operations  16.6 us (2%)
  other arithmetic  9.36 us (1%)
  local copies, waits for them, and re-layouts  7.48 us (1%)
    all_gather x1, waiting for transfers between devices, body(): lax.all_gather(w_query[0], 'dp', axis=0, tiled=True)  222 us
    all_gather x1, waiting for transfers between devices, body(): lax.all_gather(w_out[0], 'dp', axis=1, tiled=True)  212 us
    all_gather x1, waiting for transfers between devices, body(): lax.all_gather(key_matrix[0], 'dp', axis=0, tiled=True)  76.7 us
    all_gather x1, waiting for transfers between devices, body(): lax.all_gather(value_matrix[0], 'dp', axis=0, tiled=True)  69.8 us
    all_gather x1, blocking collectives, body(): lax.all_gather(passage_vectors, 'dp', axis=0, tiled=True)  31.2 us
    dot_general x3, matrix products, body(): jnp.dot(normed, piece, preferred_element_type=jnp.float32)  16.7 us
  transfers between devices with their start and end apart: 6, of which 5 were waited for; matrix products, arithmetic and copies ran while one was open for 4% of the time, Pallas kernels for 0%

commit v1 on v0

--- a/solution.py
+++ b/solution.py
@@ -73,6 +73,27 @@
     lengths,
     teacher,
 ):
+
+    def apply_ratios_by_axis(local_array, group_axis):
+        work_now, heard, row_out = (
+            jax.lax.axis_size(group_axis),
+            jax.lax.axis_index(group_axis),
+            local_array.shape[0],
+        )
+        cards = tuple(((i, (i + 1) % work_now) for i in range(work_now)))
+        top = local_array
+        built = jnp.zeros(
+            (*local_array.shape[:0], work_now * row_out, *local_array.shape[1:]), local_array.dtype
+        )
+        j = 0
+        while j < work_now:
+            now = (heard - j) % work_now
+            built = lax.dynamic_update_slice_in_dim(built, top, now * row_out, axis=0)
+            if j < work_now - 1:
+                top = jax.lax.ppermute(top, group_axis, cards)
+            j = j + 1
+        return built
+
     query_rows = query_states[0]
     passage_rows = passage_hidden_states[0]
     query_count = query_rows.shape[0]
@@ -89,7 +110,7 @@
     pieces = (
         lax.all_gather(w_query[0], "dp", axis=0, tiled=True),
         lax.all_gather(key_matrix[0], "dp", axis=0, tiled=True),
-        lax.all_gather(value_matrix[0], "dp", axis=0, tiled=True),
+        apply_ratios_by_axis(value_matrix[0], "dp"),
     )
     queries, keys, unprojected_values = tuple(
         (jnp.dot(normed, piece, preferred_element_type=jnp.float32) for piece in pieces)

time: 715 us -> 686 us (0.959)
  waiting for transfers between devices: 593 us -> 548 us
  local copies, waits for them, and re-layouts: 7.48 us -> 19.8 us
    ppermute x0 -> x7, waiting for transfers between devices: none -> 145 us  [apply_ratios_by_axis(): top = jax.lax.ppermute(top, group_axis, cards)]
    all_gather x1, waiting for transfers between devices: 76.7 us -> 0.01 us  [body(): lax.all_gather(key_matrix[0], 'dp', axis=0, tiled=True)]
    all_gather x1 -> x0, waiting for transfers between devices: 69.8 us -> none  [body(): lax.all_gather(value_matrix[0], 'dp', axis=0, tiled=True)]
    all_gather x1, waiting for transfers between devices: 222 us -> 190 us  [body(): lax.all_gather(w_query[0], 'dp', axis=0, tiled=True)]
    all_gather x1, waiting for transfers between devices: 9.89 us -> 0.01 us  [body(): normed = lax.all_gather(normed_local, 'tensor', axis=1, tiled=True)]
    dynamic_update_slice x0 -> x8, local copies, waits for them, and re-layouts: none -> 8.86 us  [apply_ratios_by_axis(): built = lax.dynamic_update_slice_in_dim(built, top, now * row_out, axis=0)]
  transfers between devices with their start and end apart: 6 -> 12, of which waited for: 5 -> 9; matrix products, arithmetic and copies ran while one was open for 4% -> 6% of each run, Pallas kernels for 0% -> 0%
where the time goes in v1:
time: 686 us; the launch traced here: 685 us
  waiting for transfers between devices  548 us (80%)
  blocking collectives  55.6 us (8%)
  matrix products  32.4 us (5%)
  local copies, waits for them, and re-layouts  19.8 us (3%)
  between operations  16.5 us (2%)
  other arithmetic  9.39 us (1%)
    all_gather x1, waiting for transfers between devices, body(): lax.all_gather(w_out[0], 'dp', axis=1, tiled=True)  211 us
    all_gather x1, waiting for transfers between devices, body(): lax.all_gather(w_query[0], 'dp', axis=0, tiled=True)  190 us
    ppermute x7, waiting for transfers between devices, apply_ratios_by_axis(): top = jax.lax.ppermute(top, group_axis, cards)  145 us
    all_gather x1, blocking collectives, body(): lax.all_gather(passage_vectors, 'dp', axis=0, tiled=True)  31.2 us
    dot_general x3, matrix products, body(): jnp.dot(normed, piece, preferred_element_type=jnp.float32)  16.8 us
  transfers between devices with their start and end apart: 12, of which 9 were waited for; matrix products, arithmetic and copies ran while one was open for 6% of the time, Pallas kernels for 0%

profile of v1, /device:TPU:0, one launch (start us, length us, event | category | flops | bytes accessed | tf_op | source)
XLA Modules:
  0.0 685.2 jit_solution(6613265457260279007)
XLA Ops:
  8.7 2.6 psum.28
  11.3 2.4 fusion.11
  15.9 2.9 collective-permute-start
  18.8 15.3 %collective-permute-done = bf16[512,512]{1,0:T(8,128)(2,1)S(1)} collective-permute-done((bf16[512,512]{1,0:T(8,128)(2,1)S(1)}, bf16[512,512]{1,0:T(8,128)(2,1)S(1)}, u32[]{:S(2)}, u32[]{:S(2)}) %collective-permute-start) | collective-permute-done | bytes 524320 | tf_op jit(solution)/shard_map/ppermute | solution.py:93
  34.1 23.6 %collective-permute-done.1 = bf16[512,512]{1,0:T(8,128)(2,1)S(1)} collective-permute-done((bf16[512,512]{1,0:T(8,128)(2,1)S(1)}, bf16[512,512]{1,0:T(8,128)(2,1)S(1)}, u32[]{:S(2)}, u32[]{:S(2)}) %collective-permute-start.1) | collective-permute-done | bytes 524320 | tf_op jit(solution)/shard_map/ppermute | solution.py:93
  57.7 20.7 %collective-permute-done.2 = bf16[512,512]{1,0:T(8,128)(2,1)S(1)} collective-permute-done((bf16[512,512]{1,0:T(8,128)(2,1)S(1)}, bf16[512,512]{1,0:T(8,128)(2,1)S(1)}, u32[]{:S(2)}, u32[]{:S(2)}) %collective-permute-start.2) | collective-permute-done | bytes 524320 | tf_op jit(solution)/shard_map/ppermute | solution.py:93
  78.4 27.9 %collective-permute-done.3 = bf16[512,512]{1,0:T(8,128)(2,1)S(1)} collective-permute-done((bf16[512,512]{1,0:T(8,128)(2,1)S(1)}, bf16[512,512]{1,0:T(8,128)(2,1)S(1)}, u32[]{:S(2)}, u32[]{:S(2)}) %collective-permute-start.3) | collective-permute-done | bytes 524320 | tf_op jit(solution)/shard_map/ppermute | solution.py:93
  107.6 26.3 %collective-permute-done.4 = bf16[512,512]{1,0:T(8,128)(2,1)} collective-permute-done((bf16[512,512]{1,0:T(8,128)(2,1)S(1)}, bf16[512,512]{1,0:T(8,128)(2,1)}, u32[]{:S(2)}, u32[]{:S(2)}) %collective-permute-start.4) | collective-permute-done | bytes 524320 | tf_op jit(solution)/shard_map/ppermute | solution.py:93
  134.1 2.2 broadcast_in_dim.34
  138.0 11.4 %collective-permute-done.5 = bf16[512,512]{1,0:T(8,128)(2,1)} collective-permute-done((bf16[512,512]{1,0:T(8,128)(2,1)}, bf16[512,512]{1,0:T(8,128)(2,1)}, u32[]{:S(2)}, u32[]{:S(2)}) %collective-permute-start.5) | collective-permute-done | bytes 524320 | tf_op jit(solution)/shard_map/ppermute | solution.py:93
  152.0 2.0 constant_dynamic-update-slice_fusion.2
  153.9 1.9 constant_dynamic-update-slice_fusion.1
  155.8 19.5 %collective-permute-done.6 = bf16[512,512]{1,0:T(8,128)(2,1)S(1)} collective-permute-done((bf16[512,512]{1,0:T(8,128)(2,1)}, bf16[512,512]{1,0:T(8,128)(2,1)S(1)}, u32[]{:S(2)}, u32[]{:S(2)}) %collective-permute-start.6) | collective-permute-done | bytes 524320 | tf_op jit(solution)/shard_map/ppermute | solution.py:93
  176.1 4.0 convolution_convert_fusion.1
  181.0 4.1 fusion.7
  185.9 190.3 %all-gather.12.cloned.1.call-done = bf16[1,4096,2048]{2,1,0:T(8,128)(2,1)} async-done(((bf16[1,512,2048]{2,1,0:T(8,128)(2,1)}), bf16[1,4096,2048]{2,1,0:T(8,128)(2,1)}) %all-gather.12.cloned.1.call-update) | async-done | bytes 16777232 | tf_op jit(solution)/shard_map/all_gather | solution.py:111
  376.2 8.6 %fusion.2 = f32[244,2048]{1,0:T(8,128)S(1)} fusion(bf16[244,4096]{1,0:T(8,128)(2,1)} %all-gather.8.cloned.1.call-done, bf16[1,4096,2048]{2,1,0:T(8,128)(2,1)} %all-gather.12.cloned.1.call-done), kind=kOutput, calls=%fused_computation.2 | convolution fusion | flops 4093640704 | bytes 20774912 | tf_op jit(solution)/shard_map/dot_general | solution.py:116
  392.7 211.4 %all-gather.14.cloned.1.call-done = bf16[1,2048,4096]{2,1,0:T(8,128)(2,1)} async-done(((bf16[1,2048,512]{2,1,0:T(8,128)(2,1)}), bf16[1,2048,4096]{2,1,0:T(8,128)(2,1)}) %all-gather.14.cloned.1.call-update) | async-done | bytes 16777232 | tf_op jit(solution)/shard_map/all_gather | solution.py:142
  604.1 11.6 %fusion.4 = bf16[244,4096]{1,0:T(8,128)(2,1)} fusion(bf16[1,2048,4096]{2,1,0:T(8,128)(2,1)} %all-gather.14.cloned.1.call-done, bf16[180,2048]{1,0:T(8,128)(2,1)S(1)} %convert_element_type.173, bf16[64,2048]{1,0:T(8,128)(2,1)S(1)} %convert_element_type.167), kind=kOutput, calls=%fused_computation.4 | convolution fusion | flops 4096638976 | bytes 19775488 | tf_op jit(solution)/shard_map/dot_general | solution.py:140
  617.9 9.4 %all-reduce = s32[8]{0:T(128)S(1)} all-reduce(s32[8]{0:T(128)S(1)} %dynamic-update-slice), channel_id=1, replica_groups=mesh['dp'=8,'pipe'=2,'tensor'=2] {'dp'}, use_global_device_ids=true, to_apply=%add | all-reduce | flops 8 | bytes 64
  628.7 1.6 fusion.12
  630.7 3.6 psum.29
  636.3 8.8 %all-reduce.1 = (bf16[1,180,128]{2,1,0:T(8,128)(2,1)S(1)}, bf16[2,32,128]{2,1,0:T(8,128)(2,1)S(1)}) all-reduce(bf16[1,180,128]{2,1,0:T(8,128)(2,1)S(1)} %fusion.49, bf16[2,32,128]{2,1,0:T(8,128)(2,1)S(1)} %bitcast.116), channel_id=1, replica_groups=mesh['dp'=8,'pipe'=2,'tensor'=2] {'pipe'}, use_global_device_ids=true, to_apply=%region_8.9 | all-reduce | flops 31232 | bytes 124928 | tf_op jit(solution)/shard_map/psum | solution.py:18
  645.1 31.2 %all_gather.23 = bf16[8,180,128]{2,1,0:T(8,128)(2,1)S(1)} all-gather(bf16[1,180,128]{2,1,0:T(8,128)(2,1)S(1)} %get-tuple-element.4), channel_id=1, replica_groups=mesh['dp'=8,'pipe'=2,'tensor'=2] {'dp'}, dimensions={0}, use_global_device_ids=true | all-gather | bytes 414720 | tf_op jit(solution)/shard_map/all_gather | solution.py:170
  (108 shorter events, 25.4 us)
Async XLA Ops:
  7.2 623.1 %copy-start = (bf16[2048,128]{1,0:T(8,128)(2,1)S(1)}, bf16[2048,128]{1,0:T(8,128)(2,1)}, u32[]{:S(2)}) copy-start(bf16[2048,128]{1,0:T(8,128)(2,1)} %param.17) | copy-start | bytes 1572868
  7.2 169.0 %all-gather.8.cloned.1.call-start = ((), (), s32[]{:S(2)}) async-start(), calls=%async_computation.1 | async-start | bytes 3047424 | tf_op jit(solution)/shard_map/all_gather | solution.py:107
  13.8 167.2 %all-gather.10.cloned.1.call-start = ((), (), s32[]{:S(2)}) async-start(), calls=%async_computation.3 | async-start | bytes 4718592 | tf_op jit(solution)/shard_map/all_gather | solution.py:112
  14.5 1.4 copy-start.4
  14.5 361.7 %all-gather.12.cloned.1.call-start = ((), (), s32[]{:S(2)}) async-start(), calls=%async_computation.4 | async-start | bytes 18874368 | tf_op jit(solution)/shard_map/all_gather | solution.py:111
  15.2 588.8 %all-gather.14.cloned.1.call-start = ((), (), s32[]{:S(2)}) async-start(), calls=%async_computation.5 | async-start | bytes 18874368 | tf_op jit(solution)/shard_map/all_gather | solution.py:142
  15.8 612.9 %reduce-scatter.2.cloned.1.call-start = ((), (), s32[]{:S(2)}) async-start(), calls=%async_computation.2 | async-start | bytes 3047424 | tf_op jit(solution)/shard_map/reduce_scatter | solution.py:145
  15.9 18.2 %collective-permute-start = (bf16[512,512]{1,0:T(8,128)(2,1)S(1)}, bf16[512,512]{1,0:T(8,128)(2,1)S(1)}, u32[]{:S(2)}, u32[]{:S(2)}) collective-permute-start(bf16[512,512]{1,0:T(8,128)(2,1)S(1)} %bitcast.113), channel_id=1, source_target_pairs={{0,4},{4,8},{8,12},{12,16},{16,20},{20,24},{24,28},{28,0},{1,5},{5... | collective-permute-start | bytes 1572872 | tf_op jit(solution)/shard_map/ppermute | solution.py:93
  34.0 23.6 %collective-permute-start.1 = (bf16[512,512]{1,0:T(8,128)(2,1)S(1)}, bf16[512,512]{1,0:T(8,128)(2,1)S(1)}, u32[]{:S(2)}, u32[]{:S(2)}) collective-permute-start(bf16[512,512]{1,0:T(8,128)(2,1)S(1)} %collective-permute-done), channel_id=1, source_target_pairs={{0,4},{4,8},{8,12},{12,16},{16,20},{20,24},{24,28},{28,0},{1,5},{5... | collective-permute-start | bytes 1572872 | tf_op jit(solution)/shard_map/ppermute | solution.py:93
  57.7 20.7 %collective-permute-start.2 = (bf16[512,512]{1,0:T(8,128)(2,1)S(1)}, bf16[512,512]{1,0:T(8,128)(2,1)S(1)}, u32[]{:S(2)}, u32[]{:S(2)}) collective-permute-start(bf16[512,512]{1,0:T(8,128)(2,1)S(1)} %collective-permute-done.1), channel_id=1, source_target_pairs={{0,4},{4,8},{8,12},{12,16},{16,20},{20,24},{24,28},{28,0},{1,5},{5... | collective-permute-start | bytes 1572872 | tf_op jit(solution)/shard_map/ppermute | solution.py:93
  78.4 27.9 %collective-permute-start.3 = (bf16[512,512]{1,0:T(8,128)(2,1)S(1)}, bf16[512,512]{1,0:T(8,128)(2,1)S(1)}, u32[]{:S(2)}, u32[]{:S(2)}) collective-permute-start(bf16[512,512]{1,0:T(8,128)(2,1)S(1)} %collective-permute-done.2), channel_id=1, source_target_pairs={{0,4},{4,8},{8,12},{12,16},{16,20},{20,24},{24,28},{28,0},{1,5},{5... | collective-permute-start | bytes 1572872 | tf_op jit(solution)/shard_map/ppermute | solution.py:93
  106.3 27.6 %collective-permute-start.4 = (bf16[512,512]{1,0:T(8,128)(2,1)S(1)}, bf16[512,512]{1,0:T(8,128)(2,1)}, u32[]{:S(2)}, u32[]{:S(2)}) collective-permute-start(bf16[512,512]{1,0:T(8,128)(2,1)S(1)} %collective-permute-done.3), channel_id=1, source_target_pairs={{0,4},{4,8},{8,12},{12,16},{16,20},{20,24},{24,28},{28,0},{1,5},{5... | collective-permute-start | bytes 1572872 | tf_op jit(solution)/shard_map/ppermute | solution.py:93
  133.9 15.5 %collective-permute-start.5 = (bf16[512,512]{1,0:T(8,128)(2,1)}, bf16[512,512]{1,0:T(8,128)(2,1)}, u32[]{:S(2)}, u32[]{:S(2)}) collective-permute-start(bf16[512,512]{1,0:T(8,128)(2,1)} %collective-permute-done.4), channel_id=1, source_target_pairs={{0,4},{4,8},{8,12},{12,16},{16,20},{20,24},{24,28},{28,0},{1,5},{5... | collective-permute-start | bytes 1572872 | tf_op jit(solution)/shard_map/ppermute | solution.py:93
  136.4 14.7 %copy-start.6 = (bf16[512,512]{1,0:T(8,128)(2,1)S(1)}, bf16[512,512]{1,0:T(8,128)(2,1)}, u32[]{:S(2)}) copy-start(bf16[512,512]{1,0:T(8,128)(2,1)} %copy-done.5) | copy-start | bytes 1572868
  149.4 25.9 %collective-permute-start.6 = (bf16[512,512]{1,0:T(8,128)(2,1)}, bf16[512,512]{1,0:T(8,128)(2,1)S(1)}, u32[]{:S(2)}, u32[]{:S(2)}) collective-permute-start(bf16[512,512]{1,0:T(8,128)(2,1)} %collective-permute-done.5), channel_id=1, source_target_pairs={{0,4},{4,8},{8,12},{12,16},{16,20},{20,24},{24,28},{28,0},{1,5},{5... | collective-permute-start | bytes 1572872 | tf_op jit(solution)/shard_map/ppermute | solution.py:93
  384.9 1.3 copy-start.2
  386.7 1.4 slice-start
  389.6 1.3 copy-start.7
  615.7 0.8 copy-start.11
  615.7 11.6 %copy-start.8 = (bf16[2048]{0:T(1024)(128)(2,1)S(1)}, bf16[2048]{0:T(1024)(128)(2,1)}, u32[]{:S(2)}) copy-start(bf16[2048]{0:T(1024)(128)(2,1)} %param.16) | copy-start | bytes 12292
  615.7 11.6 %copy-start.10 = (f32[1,8]{1,0:T(1,128)S(1)}, f32[1,8]{1,0:T(1,128)}, u32[]{:S(2)}) copy-start(f32[1,8]{1,0:T(1,128)} %param.19) | copy-start | bytes 100
  615.7 13.0 %copy-start.1 = (bf16[1,180,2048]{2,1,0:T(8,128)(2,1)S(1)}, bf16[1,180,2048]{2,1,0:T(8,128)(2,1)}, u32[]{:S(2)}) copy-start(bf16[1,180,2048]{2,1,0:T(8,128)(2,1)} %param.11) | copy-start | bytes 2211844
  615.7 13.0 %copy-start.3 = (bf16[1,64,2048]{2,1,0:T(8,128)(2,1)S(1)}, bf16[1,64,2048]{2,1,0:T(8,128)(2,1)}, u32[]{:S(2)}) copy-start(bf16[1,64,2048]{2,1,0:T(8,128)(2,1)} %param.10) | copy-start | bytes 786436
  676.8 1.9 copy-start.9
  (1 other events, 0.8 us)
Sparse Core Ops, SparseCore 0:
  13.9 13.0 all-gather.7
  29.1 101.8 all-gather.9
  133.1 243.0 all-gather.11
  378.1 225.9 all-gather.13
  615.9 7.7 reduce-scatter.1
